TPU v7x, 256 devices: a whole 4x4x8 slice. The times are simulated.
256 devices in a mesh: ctx: 16 (over y, x), head: 8 (over z), pipe: 2 (over core).
Axes of the slice: x: 4, y: 4, z: 8, core: 2. Of those that a mesh axis runs over, the one named last changes fastest.
Arguments:
- queries: bfloat16 [2, 2048, 8192], P('pipe', 'ctx', 'head'), may hold values from -6 to 6
- keys: bfloat16 [2, 2048, 8192], P('pipe', 'ctx', 'head'), may hold values from -6 to 6
- values: bfloat16 [2, 2048, 8192], P('pipe', 'ctx', 'head'), may hold values from -6 to 6
- gates: bfloat16 [2, 2048, 8192], P('pipe', 'ctx', 'head'), may hold values from -6 to 6
- log_decay: float32 [2, 2048, 64], P('pipe', 'ctx', 'head'), may hold values from -1 to 0
- segment_ids: int32 [2, 2048], P('pipe', 'ctx'), may hold values from 0 to 7, never falling along the last dimension, each value on 1 to 512 neighbouring positions
- norm_gain: float32 [2, 8192], P('pipe', 'head'), may hold values from 0.1 to 1.9
- out_weight: bfloat16 [2, 8192, 6144], P('pipe', 'head', 'ctx'), may hold values from -0.0625 to 0.0625
Outputs:
- handed: bfloat16 [2, 2048, 6144], P('pipe', 'ctx', 'head')
Inputs may be any that keep to these rules, and one draw needn't show every extreme that they name: `segment_ids`: along each section's tokens the ids never fall; a document has at most a quarter of 2048 tokens, and one has exactly that many.
All inputs are finite; a program needn't handle non-finite values.
Results may differ from a plain program's by a relative error of at most 0.02.
Values may be sent and summed in bfloat16 or wider, within the bound.
A program may use at most 64 MiB of HBM per device.

v0:
```python
import jax
import jax.numpy as jnp
from jax import lax
from jax.sharding import PartitionSpec as P

DH = 128
highest = lax.Precision.HIGHEST


def entering(shard, axis, combine, identity):
    count, index = (lax.axis_size(axis), lax.axis_index(axis))
    everything = jax.tree.map(
        lambda part, kind: lax.all_gather(part.astype(kind), axis),
        shard,
        (jnp.bfloat16, jnp.bfloat16, jnp.bfloat16),
    )
    start = jax.tree.map(
        lambda part, zero: jnp.broadcast_to(jnp.asarray(zero, part.dtype), part.shape),
        shard,
        identity,
    )

    def hop(k, before):
        reached = k < index
        new = combine(
            before, jax.tree.map(lambda part, own: part[k].astype(own.dtype), everything, shard)
        )
        return jax.tree.map(lambda a, b: jnp.where(reached, a, b), new, before)

    return lax.fori_loop(0, count, hop, start)


def from_behind(shard, axis, by):
    count = lax.axis_size(axis)
    return lax.ppermute(shard, axis, [(i, (i + by) % count) for i in range(count)])


def block_step(carried, pieces):
    kv_state, doc_id = carried
    query_rows, key_rows, value_rows, rate_rows, doc_rows = pieces
    length = doc_rows.shape[0]
    running = jnp.cumsum(rate_rows, axis=0)
    running_t = running.T
    causal = lax.broadcasted_iota(jnp.int32, (length, length), 0) >= lax.broadcasted_iota(
        jnp.int32, (length, length), 1
    )
    allowed = causal & (doc_rows[:, None] == doc_rows[None, :])
    log_gaps = running_t[:, :, None] - running_t[:, None, :]
    weights = jnp.where(allowed[None], jnp.exp(jnp.where(allowed[None], log_gaps, 0.0)), 0.0)
    scores = jnp.einsum("ihd,jhd->hij", query_rows, key_rows, preferred_element_type=jnp.float32)
    mixed = (scores * weights).astype(jnp.bfloat16)
    inside = jnp.einsum("hij,jhd->ihd", mixed, value_rows, preferred_element_type=jnp.float32)
    value_full = value_rows.astype(jnp.float32)
    reaches = jnp.exp(running) * (doc_rows == doc_id).astype(jnp.float32)[:, None]
    carried_part = jnp.einsum(
        "ihd,hde->ihe",
        query_rows.astype(jnp.float32) * reaches[:, :, None],
        kv_state,
        precision=highest,
    )
    final_doc = doc_rows[-1]
    retain = (doc_id == final_doc).astype(jnp.float32)
    fading = (
        jnp.exp(running[-1][None, :] - running)
        * (doc_rows == final_doc).astype(jnp.float32)[:, None]
    )
    fresh_part = jnp.einsum(
        "jhd,jhe->hde",
        key_rows.astype(jnp.float32) * fading[:, :, None],
        value_full,
        precision=highest,
    )
    new_state = retain * jnp.exp(running[-1])[:, None, None] * kv_state + fresh_part
    return ((new_state, final_doc), inside + carried_part)


def sweep(query3, key3, value3, rate_rows, doc_rows, start_state, start_doc):
    rows_here = doc_rows.shape[0]
    heads_here = query3.shape[1]
    block_len = min(512, rows_here)
    block_count = rows_here // block_len
    pieces = (
        query3.reshape(block_count, block_len, heads_here, DH),
        key3.reshape(block_count, block_len, heads_here, DH),
        value3.reshape(block_count, block_len, heads_here, DH),
        rate_rows.reshape(block_count, block_len, heads_here),
        doc_rows.reshape(block_count, block_len),
    )
    final_carry, attended = lax.scan(block_step, (start_state, start_doc), pieces)
    return (final_carry[0], attended.reshape(rows_here, heads_here, DH))


def combine_pair(earlier, later):
    rate_early, state_early, doc_early = earlier
    rate_late, state_late, doc_late = later
    linked = ((doc_early == doc_late) | (doc_early < 0) | (doc_late < 0)).astype(jnp.float32)
    merged = linked[0] * rate_late[:, None, None] * state_early + state_late
    return (rate_early * rate_late, merged, jnp.where(doc_late < 0, doc_early, doc_late))


def carry_in(shard_rates, shard_state, shard_doc):
    heads_here = shard_rates.shape[0]
    neutral = (
        jnp.ones((heads_here,), jnp.float32),
        jnp.zeros((heads_here, DH, DH), jnp.float32),
        jnp.full((1,), -1.0, jnp.float32),
    )
    prefix = entering((shard_rates, shard_state, shard_doc), "ctx", combine_pair, neutral)
    return (prefix[1], prefix[2])


def on_device(queries, keys, values, gates, log_decay, segment_ids, norm_gain, out_weight):
    rows_here = queries.shape[1]
    width = queries.shape[2]
    heads_here = width // DH
    query3 = queries[0].reshape(rows_here, heads_here, DH)
    key3 = keys[0].reshape(rows_here, heads_here, DH)
    value3 = values[0].reshape(rows_here, heads_here, DH)
    rate_rows = log_decay[0]
    doc_rows = segment_ids[0].astype(jnp.float32)
    running = jnp.cumsum(rate_rows, axis=0)
    shard_rates = jnp.exp(running[-1])
    shard_doc = doc_rows[-1:]
    fading = (
        jnp.exp(running[-1][None, :] - running)
        * (doc_rows == shard_doc[0]).astype(jnp.float32)[:, None]
    )
    shard_state = jnp.einsum(
        "jhd,jhe->hde",
        key3.astype(jnp.float32) * fading[:, :, None],
        value3.astype(jnp.float32),
        precision=highest,
    )
    incoming, incoming_doc = carry_in(shard_rates, shard_state, shard_doc)
    ignored, attended = sweep(query3, key3, value3, rate_rows, doc_rows, incoming, incoming_doc[0])
    scaling = lax.rsqrt(jnp.mean(attended * attended, axis=-1, keepdims=True) + 1e-06)
    normed = (
        (attended * scaling).reshape(rows_here, width)
        * norm_gain[0][None, :]
        * jax.nn.sigmoid(gates[0].astype(jnp.float32))
    ).astype(jnp.bfloat16)
    weight_here = out_weight[0]
    partial_value = jnp.dot(
        normed,
        lax.all_gather(weight_here, "ctx", axis=1, tiled=True),
        preferred_element_type=jnp.float32,
    )
    summed = lax.psum_scatter(
        partial_value.astype(jnp.bfloat16), "head", scatter_dimension=1, tiled=True
    )
    handed = from_behind(summed, "pipe", 1)
    return handed[None]


def solution(mesh):
    return jax.shard_map(
        on_device,
        mesh=mesh,
        in_specs=(
            P("pipe", "ctx", "head"),
            P("pipe", "ctx", "head"),
            P("pipe", "ctx", "head"),
            P("pipe", "ctx", "head"),
            P("pipe", "ctx", "head"),
            P("pipe", "ctx"),
            P("pipe", "head"),
            P("pipe", "head", "ctx"),
        ),
        out_specs=P("pipe", "ctx", "head"),
        check_vma=False,
    )
```

profile of v0, /device:TPU:1, one launch (start us, length us, event | category | flops | bytes accessed | tf_op | source)
XLA Modules:
  0.0 237.9 jit_solution(17835527506379368174)
XLA Ops:
  8.8 1.3 compare_convert_fusion.1
  10.2 1.1 copy.36
  12.3 1.1 convolution_convert_fusion
  15.0 1.3 dynamic-slice.1
  17.0 34.4 %all-reduce = bf16[16]{0:T(256)(128)(2,1)S(1)} all-reduce(bf16[16]{0:T(256)(128)(2,1)S(1)} %dynamic-update-slice), channel_id=1, replica_groups=mesh['ctx'=16,'head'=8,'pipe'=2] {'ctx'}, use_global_device_ids=true, to_apply=%add | all-reduce | flops 16 | bytes 64
  51.4 14.6 %all-gather.2 = bf16[16,1,8]{2,1,0:T(2,128)(2,1)S(1)} all-gather(bf16[1,1,8]{2,1,0:T(2,128)(2,1)S(1)} %get-tuple-element.212), channel_id=1, replica_groups=mesh['ctx'=16,'head'=8,'pipe'=2] {'ctx'}, dimensions={0}, use_global_device_ids=true | all-gather | bytes 272 | tf_op jit(solution)/shard_map/all_gather | solution.py:13
  67.1 7.1 %all-gather.6.cloned.1.call-done = bf16[128,128,128]{2,1,0:T(8,128)(2,1)} async-done(((bf16[8,128,128]{2,1,0:T(8,128)(2,1)}), bf16[128,128,128]{2,1,0:T(8,128)(2,1)}) %all-gather.6.cloned.1.call-update) | async-done | bytes 4194320 | tf_op jit(solution)/shard_map/all_gather | solution.py:13
  74.2 62.4 %while.10 = (s32[]{:T(128)}, f32[8,128,128]{2,1,0:T(8,128)S(1)}, f32[1]{0:T(128)}, s32[]{:T(128)}, bf16[16,1]{0,1:T(2,128)(2,1)S(1)}, /*index=5*/bf16[16,8]{1,0:...) while((s32[]{:T(128)}, f32[8,128,128]{2,1,0:T(8,128)S(1)}, ...), condition=%wide.region_2.3_spmd.clone, body=%wide.region_1.2_spmd.clone.sunk | while | flops 655388 | bytes 1310999 | solution.py:30
  76.3 1.1 fusion.44
  80.2 1.1 fusion.44
  84.1 1.1 fusion.44
  88.0 1.1 fusion.44
  91.9 1.1 fusion.44
  95.8 1.1 fusion.44
  99.7 1.1 fusion.44
  103.6 1.1 fusion.44
  123.1 1.1 fusion.44
  127.0 1.1 fusion.44
  136.8 1.3 convolution_bitcast_fusion.1
  138.9 41.3 %all-gather.8.cloned.1.call-done = bf16[1,1024,6144]{2,1,0:T(8,128)(2,1)} async-done(((bf16[1,1024,384]{2,1,0:T(8,128)(2,1)}), bf16[1,1024,6144]{2,1,0:T(8,128)(2,1)}) %all-gather.8.cloned.1.call-update) | async-done | bytes 12582928 | tf_op jit(solution)/shard_map/all_gather | solution.py:145
  180.1 7.6 %fusion.6 = bf16[128,6144]{1,0:T(8,128)(2,1)} fusion(bf16[1,1024,6144]{2,1,0:T(8,128)(2,1)} %all-gather.8.cloned.1.call-done, bf16[1,128,1024]{2,1,0:T(8,128)(2,1)S(1)} %copy-done, f32[128,1024]{1,0:T(8,128)S(1)} %copy.34, f32[1024]{0:T(1024)S(1)} %bitcast.81), kind=kOutput, calls=%fused_computation.9 | convolution fusion | flops 1612316672 | bytes 14946304 | tf_op jit(solution)/shard_map/dot_general | solution.py:143
  187.8 37.0 %reduce-scatter.2.cloned.1.call-done = bf16[128,768]{1,0:T(8,128)(2,1)} async-done(((bf16[128,6144]{1,0:T(8,128)(2,1)}), bf16[128,768]{1,0:T(8,128)(2,1)}) %reduce-scatter.2.cloned.1.call-update) | async-done | bytes 196624 | tf_op jit(solution)/shard_map/reduce_scatter | solution.py:148
  224.8 4.6 %collective-permute-start = (bf16[128,768]{1,0:T(8,128)(2,1)}, bf16[128,768]{1,0:T(8,128)(2,1)S(1)}, u32[]{:S(2)}, u32[]{:S(2)}) collective-permute-start(bf16[128,768]{1,0:T(8,128)(2,1)} %reduce-scatter.2.cloned.1.call-done), channel_id=1, source_target_pairs={{0,1},{1,0},{2,3},{3,2},{4,5},{5,4},{6,7},{7,6},{8,9},{9,8},{10,11... | collective-permute-start | bytes 589832 | tf_op jit(solution)/shard_map/ppermute | solution.py:35
  229.4 1.3 collective-permute-done
  (73 shorter events, 25.0 us)
Async XLA Ops:
  6.5 67.7 %all-gather.6.cloned.1.call-start = ((), (), s32[]{:S(2)}) async-start(), calls=%async_computation.2 | async-start | bytes 4456448 | tf_op jit(solution)/shard_map/all_gather | solution.py:13
  13.5 123.2 %copy-start.2 = (s32[1,128]{1,0:T(1,128)S(1)}, s32[1,128]{1,0:T(1,128)}, u32[]{:S(2)}) copy-start(s32[1,128]{1,0:T(1,128)} %param.15) | copy-start | bytes 1540
  13.5 166.6 %all-gather.8.cloned.1.call-start = ((), (), s32[]{:S(2)}) async-start(), calls=%async_computation.3 | async-start | bytes 13369344 | tf_op jit(solution)/shard_map/all_gather | solution.py:145
  14.2 210.5 %reduce-scatter.2.cloned.1.call-start = ((), (), s32[]{:S(2)}) async-start(), calls=%async_computation.1 | async-start | bytes 1769472 | tf_op jit(solution)/shard_map/reduce_scatter | solution.py:148
  136.6 43.5 %copy-start = (bf16[1,128,1024]{2,1,0:T(8,128)(2,1)S(1)}, bf16[1,128,1024]{2,1,0:T(8,128)(2,1)}, u32[]{:S(2)}) copy-start(bf16[1,128,1024]{2,1,0:T(8,128)(2,1)} %param.13) | copy-start | bytes 786436
  136.6 43.5 %copy-start.1 = (f32[1,1024]{1,0:T(1,128)S(1)}, f32[1,1024]{1,0:T(1,128)}, u32[]{:S(2)}) copy-start(f32[1,1024]{1,0:T(1,128)} %param.16) | copy-start | bytes 12292
  224.8 5.9 %collective-permute-start = (bf16[128,768]{1,0:T(8,128)(2,1)}, bf16[128,768]{1,0:T(8,128)(2,1)S(1)}, u32[]{:S(2)}, u32[]{:S(2)}) collective-permute-start(bf16[128,768]{1,0:T(8,128)(2,1)} %reduce-scatter.2.cloned.1.call-done), channel_id=1, source_target_pairs={{0,1},{1,0},{2,3},{3,2},{4,5},{5,4},{6,7},{7,6},{8,9},{9,8},{10,11... | collective-permute-start | bytes 589832 | tf_op jit(solution)/shard_map/ppermute | solution.py:35
Sparse Core Ops, SparseCore 0:
  13.6 60.5 all-gather.5
  76.6 103.4 all-gather.7
  187.9 36.8 reduce-scatter.1
where the time goes:
time: 239 us; the launch traced here: 238 us
  waiting for transfers between devices  87.4 us (37%)
  blocking collectives  48.9 us (20%)
  loops' own time  34.1 us (14%)
  other arithmetic  20.2 us (8%)
  local copies, waits for them, and re-layouts  18.2 us (8%)
  between operations  13.9 us (6%)
  matrix products  10.5 us (4%)
  starting transfers between devices  4.7 us (2%)
    all_gather x1, waiting for transfers between devices, on_device(): lax.all_gather(weight_here, 'ctx', axis=1, tiled=True)  41.3 us
    reduce_scatter x1, waiting for transfers between devices, on_device(): lax.psum_scatter(partial_value.astype(jnp.bfloat16), 'head', scatter_dime...  37 us
    unnamed x1, blocking collectives  34.4 us
    another operation x1, loops' own time, entering(): return lax.fori_loop(0, count, hop, start)  34.1 us
    select_n x16, other arithmetic, hop(): return jax.tree.map(lambda a, b: jnp.where(reached, a, b), new, before)  17.5 us
    all_gather x1, blocking collectives, entering(): lax.all_gather(part.astype(kind), axis)  14.6 us
    dynamic_slice x16, local copies, waits for them, and re-layouts, hop(): part[k].astype(own.dtype)  10.6 us
    dot_general x1, matrix products, on_device(): jnp.dot(normed, lax.all_gather(weight_here, 'ctx', axis=1, tiled=True), p...  7.63 us
  transfers between devices with their start and end apart: 4, of which 4 were waited for; matrix products, arithmetic and copies ran while one was open for 14% of the time, Pallas kernels for 0%

commit v1 on v0

--- a/solution.py
+++ b/solution.py
@@ -5,6 +5,32 @@
 
 DH = 128
 highest = lax.Precision.HIGHEST
+
+
+def resolve_blocks_for(patch, pos_dim):
+    patch = jnp.moveaxis(patch, 0, pos_dim)
+    current_arr = patch.shape
+    return patch.reshape(
+        *current_arr[:pos_dim],
+        current_arr[pos_dim] * current_arr[pos_dim + 1],
+        *current_arr[pos_dim + 2 :]
+    )
+
+
+def test_bench(v0, named_axis, dim_no):
+    how_many = lax.axis_size(named_axis)
+    block_list = [(j0, (j0 + 1) % how_many) for j0 in range(how_many)]
+    buffer = [(jj, i0) for i0, jj in block_list]
+    item_now, latest = ([], [])
+    for j in range(how_many - 1):
+        if j % 2 == 0:
+            item_now.append(lax.ppermute(item_now[-1] if item_now else v0, named_axis, block_list))
+        else:
+            latest.append(lax.ppermute(latest[-1] if latest else v0, named_axis, buffer))
+    next_value = jnp.stack([*item_now[::-1], v0, *latest])
+    back = lax.axis_index(named_axis) - len(item_now)
+    next_value = next_value[(jnp.arange(how_many) - back) % how_many]
+    return resolve_blocks_for(next_value, dim_no)
 
 
 def entering(shard, axis, combine, identity):
@@ -141,9 +167,7 @@
     ).astype(jnp.bfloat16)
     weight_here = out_weight[0]
     partial_value = jnp.dot(
-        normed,
-        lax.all_gather(weight_here, "ctx", axis=1, tiled=True),
-        preferred_element_type=jnp.float32,
+        normed, test_bench(weight_here, "ctx", 1), preferred_element_type=jnp.float32
     )
     summed = lax.psum_scatter(
         partial_value.astype(jnp.bfloat16), "head", scatter_dimension=1, tiled=True

time: 239 us -> 420 us (1.76)
  waiting for transfers between devices: 87.4 us -> 164 us
  local copies, waits for them, and re-layouts: 18.2 us -> 77.1 us
  starting transfers between devices: 4.7 us -> 40.2 us
  blocking collectives: 48.9 us -> 54.4 us
    ppermute x0 -> x15, waiting for transfers between devices: none -> 86.7 us  [the longest x8 64.3 us: test_bench(): lax.ppermute(item_now[-1] if item_now else v0, named_axis, block_list)]
    all_gather x1 -> x0, waiting for transfers between devices: 41.3 us -> none  [on_device(): lax.all_gather(weight_here, 'ctx', axis=1, tiled=True)]
    reduce_scatter x1, waiting for transfers between devices: 37 us -> 75.8 us  [on_device(): lax.psum_scatter(partial_value.astype(jnp.bfloat16), 'head', scatter_dime...]
    ppermute x0 -> x15, starting transfers between devices: none -> 35.4 us  [the longest x7 33.4 us: test_bench(): lax.ppermute(latest[-1] if latest else v0, named_axis, buffer)]
    unnamed x13 -> x48, local copies, waits for them, and re-layouts: 4.72 us -> 34.5 us
    transpose x0 -> x1, local copies, waits for them, and re-layouts: none -> 16.6 us  [resolve_blocks_for(): patch = jnp.moveaxis(patch, 0, pos_dim)]
    gather x0 -> x1, local copies, waits for them, and re-layouts: none -> 11.5 us  [test_bench(): next_value = next_value[(jnp.arange(how_many) - back) % how_many]]
    all_gather x1, waiting for transfers between devices: 7.12 us -> 0.01 us  [entering(): lax.all_gather(part.astype(kind), axis)]
  transfers between devices with their start and end apart: 4 -> 18, of which waited for: 4 -> 13; matrix products, arithmetic and copies ran while one was open for 14% -> 16% of each run, Pallas kernels for 0% -> 0%
where the time goes in v1:
time: 420 us; the launch traced here: 418 us
  waiting for transfers between devices  164 us (39%)
  local copies, waits for them, and re-layouts  77.1 us (18%)
  blocking collectives  54.4 us (13%)
  starting transfers between devices  40.2 us (10%)
  loops' own time  34 us (8%)
  other arithmetic  21.4 us (5%)
  between operations  14.3 us (3%)
  matrix products  12.9 us (3%)
    reduce_scatter x1, waiting for transfers between devices, on_device(): lax.psum_scatter(partial_value.astype(jnp.bfloat16), 'head', scatter_dime...  75.8 us
    ppermute x8, waiting for transfers between devices, test_bench(): lax.ppermute(item_now[-1] if item_now else v0, named_axis, block_list)  64.3 us
    unnamed x1, blocking collectives  37.4 us
    unnamed x48, local copies, waits for them, and re-layouts  34.5 us
    another operation x1, loops' own time, entering(): return lax.fori_loop(0, count, hop, start)  34 us
    ppermute x7, starting transfers between devices, test_bench(): lax.ppermute(latest[-1] if latest else v0, named_axis, buffer)  33.4 us
    ppermute x7, waiting for transfers between devices, test_bench(): lax.ppermute(latest[-1] if latest else v0, named_axis, buffer)  22.4 us
    select_n x16, other arithmetic, hop(): return jax.tree.map(lambda a, b: jnp.where(reached, a, b), new, before)  17.5 us
  transfers between devices with their start and end apart: 18, of which 13 were waited for; matrix products, arithmetic and copies ran while one was open for 16% of the time, Pallas kernels for 0%

profile of v1, /device:TPU:1, one launch (start us, length us, event | category | flops | bytes accessed | tf_op | source)
XLA Modules:
  0.0 418.0 jit_solution(5696145613551624040)
XLA Ops:
  8.6 19.4 %collective-permute-done = bf16[1024,384]{1,0:T(8,128)(2,1)S(1)} collective-permute-done((bf16[1024,384]{1,0:T(8,128)(2,1)}, bf16[1024,384]{1,0:T(8,128)(2,1)S(1)}, u32[]{:S(2)}, u32[]{:S(2)}) %collective-permute-start) | collective-permute-done | bytes 786464 | tf_op jit(solution)/shard_map/ppermute | solution.py:27
  28.9 4.8 %collective-permute-start.8 = (bf16[1024,384]{1,0:T(8,128)(2,1)}, bf16[1024,384]{1,0:T(8,128)(2,1)S(1)}, u32[]{:S(2)}, u32[]{:S(2)}) collective-permute-start(bf16[1024,384]{1,0:T(8,128)(2,1)} %bitcast.107), channel_id=1, source_target_pairs={{16,0},{32,16},{48,32},{64,48},{80,64},{96,80},{112,96},{128,112},... | collective-permute-start | bytes 2359304 | tf_op jit(solution)/shard_map/ppermute | solution.py:29
  33.6 14.4 %collective-permute-done.1 = bf16[1024,384]{1,0:T(8,128)(2,1)S(1)} collective-permute-done((bf16[1024,384]{1,0:T(8,128)(2,1)S(1)}, bf16[1024,384]{1,0:T(8,128)(2,1)S(1)}, u32[]{:S(2)}, u32[]{:S(2)}) %collective-permute-start.1) | collective-permute-done | bytes 786464 | tf_op jit(solution)/shard_map/ppermute | solution.py:27
  53.9 4.9 %collective-permute-start.9 = (bf16[1024,384]{1,0:T(8,128)(2,1)S(1)}, bf16[1024,384]{1,0:T(8,128)(2,1)}, u32[]{:S(2)}, u32[]{:S(2)}) collective-permute-start(bf16[1024,384]{1,0:T(8,128)(2,1)S(1)} %collective-permute-done.8), channel_id=1, source_target_pairs={{16,0},{32,16},{48,32},{64,48},{80,64},{96,80},{112,96},{128,112},... | collective-permute-start | bytes 2359304 | tf_op jit(solution)/shard_map/ppermute | solution.py:29
  58.8 7.7 %collective-permute-done.2 = bf16[1024,384]{1,0:T(8,128)(2,1)} collective-permute-done((bf16[1024,384]{1,0:T(8,128)(2,1)S(1)}, bf16[1024,384]{1,0:T(8,128)(2,1)}, u32[]{:S(2)}, u32[]{:S(2)}) %collective-permute-start.2) | collective-permute-done | bytes 786464 | tf_op jit(solution)/shard_map/ppermute | solution.py:27
  67.7 3.6 collective-permute-done.9
  71.3 5.6 %collective-permute-start.10 = (bf16[1024,384]{1,0:T(8,128)(2,1)}, bf16[1024,384]{1,0:T(8,128)(2,1)S(1)}, u32[]{:S(2)}, u32[]{:S(2)}) collective-permute-start(bf16[1024,384]{1,0:T(8,128)(2,1)} %collective-permute-done.9), channel_id=1, source_target_pairs={{16,0},{32,16},{48,32},{64,48},{80,64},{96,80},{112,96},{128,112},... | collective-permute-start | bytes 2359304 | tf_op jit(solution)/shard_map/ppermute | solution.py:29
  76.9 7.3 %collective-permute-done.3 = bf16[1024,384]{1,0:T(8,128)(2,1)} collective-permute-done((bf16[1024,384]{1,0:T(8,128)(2,1)}, bf16[1024,384]{1,0:T(8,128)(2,1)}, u32[]{:S(2)}, u32[]{:S(2)}) %collective-permute-start.3) | collective-permute-done | bytes 786464 | tf_op jit(solution)/shard_map/ppermute | solution.py:27
  84.2 4.6 %collective-permute-done.10 = bf16[1024,384]{1,0:T(8,128)(2,1)S(1)} collective-permute-done((bf16[1024,384]{1,0:T(8,128)(2,1)}, bf16[1024,384]{1,0:T(8,128)(2,1)S(1)}, u32[]{:S(2)}, u32[]{:S(2)}) %collective-permute-start.10) | collective-permute-done | bytes 786464 | tf_op jit(solution)/shard_map/ppermute | solution.py:29
  89.7 5.4 %collective-permute-start.11 = (bf16[1024,384]{1,0:T(8,128)(2,1)S(1)}, bf16[1024,384]{1,0:T(8,128)(2,1)S(1)}, u32[]{:S(2)}, u32[]{:S(2)}) collective-permute-start(bf16[1024,384]{1,0:T(8,128)(2,1)S(1)} %collective-permute-done.10), channel_id=1, source_target_pairs={{16,0},{32,16},{48,32},{64,48},{80,64},{96,80},{112,96},{128,112},... | collective-permute-start | bytes 2359304 | tf_op jit(solution)/shard_map/ppermute | solution.py:29
  95.1 8.6 %collective-permute-done.4 = bf16[1024,384]{1,0:T(8,128)(2,1)S(1)} collective-permute-done((bf16[1024,384]{1,0:T(8,128)(2,1)}, bf16[1024,384]{1,0:T(8,128)(2,1)S(1)}, u32[]{:S(2)}, u32[]{:S(2)}) %collective-permute-start.4) | collective-permute-done | bytes 786464 | tf_op jit(solution)/shard_map/ppermute | solution.py:27
  103.7 6.4 %collective-permute-done.11 = bf16[1024,384]{1,0:T(8,128)(2,1)S(1)} collective-permute-done((bf16[1024,384]{1,0:T(8,128)(2,1)S(1)}, bf16[1024,384]{1,0:T(8,128)(2,1)S(1)}, u32[]{:S(2)}, u32[]{:S(2)}) %collective-permute-start.11) | collective-permute-done | bytes 786464 | tf_op jit(solution)/shard_map/ppermute | solution.py:29
  111.0 5.5 %collective-permute-start.12 = (bf16[1024,384]{1,0:T(8,128)(2,1)S(1)}, bf16[1024,384]{1,0:T(8,128)(2,1)}, u32[]{:S(2)}, u32[]{:S(2)}) collective-permute-start(bf16[1024,384]{1,0:T(8,128)(2,1)S(1)} %collective-permute-done.11), channel_id=1, source_target_pairs={{16,0},{32,16},{48,32},{64,48},{80,64},{96,80},{112,96},{128,112},... | collective-permute-start | bytes 2359304 | tf_op jit(solution)/shard_map/ppermute | solution.py:29
  119.7 7.8 %collective-permute-done.12 = bf16[1024,384]{1,0:T(8,128)(2,1)} collective-permute-done((bf16[1024,384]{1,0:T(8,128)(2,1)S(1)}, bf16[1024,384]{1,0:T(8,128)(2,1)}, u32[]{:S(2)}, u32[]{:S(2)}) %collective-permute-start.12) | collective-permute-done | bytes 786464 | tf_op jit(solution)/shard_map/ppermute | solution.py:29
  127.5 5.6 %collective-permute-start.13 = (bf16[1024,384]{1,0:T(8,128)(2,1)}, bf16[1024,384]{1,0:T(8,128)(2,1)}, u32[]{:S(2)}, u32[]{:S(2)}) collective-permute-start(bf16[1024,384]{1,0:T(8,128)(2,1)} %collective-permute-done.12), channel_id=1, source_target_pairs={{16,0},{32,16},{48,32},{64,48},{80,64},{96,80},{112,96},{128,112},... | collective-permute-start | bytes 2359304 | tf_op jit(solution)/shard_map/ppermute | solution.py:29
  133.1 3.7 collective-permute-done.6
  139.5 37.4 %all-reduce = bf16[16]{0:T(256)(128)(2,1)S(1)} all-reduce(bf16[16]{0:T(256)(128)(2,1)S(1)} %dynamic-update-slice), channel_id=1, replica_groups=mesh['ctx'=16,'head'=8,'pipe'=2] {'ctx'}, use_global_device_ids=true, to_apply=%add | all-reduce | flops 16 | bytes 64
  176.9 17.0 %all-gather.1 = bf16[16,1,8]{2,1,0:T(2,128)(2,1)S(1)} all-gather(bf16[1,1,8]{2,1,0:T(2,128)(2,1)S(1)} %get-tuple-element.226), channel_id=1, replica_groups=mesh['ctx'=16,'head'=8,'pipe'=2] {'ctx'}, dimensions={0}, use_global_device_ids=true | all-gather | bytes 272 | tf_op jit(solution)/shard_map/all_gather | solution.py:39
  226.1 11.5 %gather_fusion = bf16[16,1024,384]{2,1,0:T(8,128)(2,1)} fusion(bf16[16,1024,384]{2,1,0:T(8,128)(2,1)} %bitcast_dynamic-update-slice_fusion, s32[1024]{0:T(1024)S(1)} %pad_clamp_fusion), kind=kCustom, calls=%fused_computation | custom fusion | bytes 25165888 | tf_op jit(solution)/shard_map/gather | solution.py:32
  237.6 16.6 %copy.66 = bf16[1024,16,384]{0,2,1:T(8,128)(2,1)} copy(bf16[1024,16,384]{2,0,1:T(8,128)(2,1)} %bitcast.96) | data formatting | bytes 25165824 | tf_op jit(solution)/shard_map/transpose | solution.py:11
  254.2 62.3 %while.10 = (s32[]{:T(128)}, f32[8,128,128]{2,1,0:T(8,128)S(1)}, f32[1]{0:T(128)}, s32[]{:T(128)}, bf16[16,1]{0,1:T(2,128)(2,1)S(1)}, /*index=5*/bf16[16,8]{1,0:...) while((s32[]{:T(128)}, f32[8,128,128]{2,1,0:T(8,128)S(1)}, ...), condition=%wide.region_2.3_spmd.clone, body=%wide.region_1.2_spmd.clone.sunk | while | flops 655388 | bytes 1310999 | solution.py:56
  318.7 10.0 %convolution_convert_fusion = bf16[128,6144]{1,0:T(8,128)(2,1)} fusion(bf16[128,1024]{0,1:T(8,128)(2,1)S(1)} %bitcast.98, bf16[1024,6144]{0,1:T(8,128)(2,1)} %bitcast.95), kind=kOutput, calls=%fused_computation.8 | convolution fusion | flops 1611399168 | bytes 14417920 | tf_op jit(solution)/shard_map/dot_general | solution.py:169
  328.8 75.8 %reduce-scatter.2.cloned.1.call-done = bf16[128,768]{1,0:T(8,128)(2,1)} async-done(((bf16[128,6144]{1,0:T(8,128)(2,1)}), bf16[128,768]{1,0:T(8,128)(2,1)}) %reduce-scatter.2.cloned.1.call-update) | async-done | bytes 196624 | tf_op jit(solution)/shard_map/reduce_scatter | solution.py:172
  404.5 4.7 %collective-permute-start.15 = (bf16[128,768]{1,0:T(8,128)(2,1)}, bf16[128,768]{1,0:T(8,128)(2,1)S(1)}, u32[]{:S(2)}, u32[]{:S(2)}) collective-permute-start(bf16[128,768]{1,0:T(8,128)(2,1)} %reduce-scatter.2.cloned.1.call-done), channel_id=1, source_target_pairs={{0,1},{1,0},{2,3},{3,2},{4,5},{5,4},{6,7},{7,6},{8,9},{9,8},{10,11... | collective-permute-start | bytes 589832 | tf_op jit(solution)/shard_map/ppermute | solution.py:61
  (141 shorter events, 81.4 us)
Async XLA Ops:
  6.5 208.3 %copy-start = (bf16[1,1024,384]{2,1,0:T(8,128)(2,1)S(1)}, bf16[1,1024,384]{2,1,0:T(8,128)(2,1)}, u32[]{:S(2)}) copy-start(bf16[1,1024,384]{2,1,0:T(8,128)(2,1)} %param.17) | copy-start | bytes 2359300
  6.5 247.7 %all-gather.4.cloned.1.call-start = ((), (), s32[]{:S(2)}) async-start(), calls=%async_computation.2 | async-start | bytes 4456448 | tf_op jit(solution)/shard_map/all_gather | solution.py:39
  6.5 21.4 %collective-permute-start = (bf16[1024,384]{1,0:T(8,128)(2,1)}, bf16[1024,384]{1,0:T(8,128)(2,1)S(1)}, u32[]{:S(2)}, u32[]{:S(2)}) collective-permute-start(bf16[1024,384]{1,0:T(8,128)(2,1)} %bitcast.106), channel_id=1, source_target_pairs={{0,16},{16,32},{32,48},{48,64},{64,80},{80,96},{96,112},{112,128},... | collective-permute-start | bytes 2359304 | tf_op jit(solution)/shard_map/ppermute | solution.py:27
  28.9 19.2 %collective-permute-start.1 = (bf16[1024,384]{1,0:T(8,128)(2,1)S(1)}, bf16[1024,384]{1,0:T(8,128)(2,1)S(1)}, u32[]{:S(2)}, u32[]{:S(2)}) collective-permute-start(bf16[1024,384]{1,0:T(8,128)(2,1)S(1)} %collective-permute-done), channel_id=1, source_target_pairs={{0,16},{16,32},{32,48},{48,64},{64,80},{80,96},{96,112},{112,128},... | collective-permute-start | bytes 2359304 | tf_op jit(solution)/shard_map/ppermute | solution.py:27
  28.9 25.0 %collective-permute-start.8 = (bf16[1024,384]{1,0:T(8,128)(2,1)}, bf16[1024,384]{1,0:T(8,128)(2,1)S(1)}, u32[]{:S(2)}, u32[]{:S(2)}) collective-permute-start(bf16[1024,384]{1,0:T(8,128)(2,1)} %bitcast.107), channel_id=1, source_target_pairs={{16,0},{32,16},{48,32},{64,48},{80,64},{96,80},{112,96},{128,112},... | collective-permute-start | bytes 2359304 | tf_op jit(solution)/shard_map/ppermute | solution.py:29
  48.1 145.8 %copy-start.4 = (bf16[1024,384]{1,0:T(8,128)(2,1)}, bf16[1024,384]{1,0:T(8,128)(2,1)S(1)}, u32[]{:S(2)}) copy-start(bf16[1024,384]{1,0:T(8,128)(2,1)S(1)} %collective-permute-done.1) | copy-start | bytes 2359300
  48.1 18.4 %collective-permute-start.2 = (bf16[1024,384]{1,0:T(8,128)(2,1)S(1)}, bf16[1024,384]{1,0:T(8,128)(2,1)}, u32[]{:S(2)}, u32[]{:S(2)}) collective-permute-start(bf16[1024,384]{1,0:T(8,128)(2,1)S(1)} %collective-permute-done.1), channel_id=1, source_target_pairs={{0,16},{16,32},{32,48},{48,64},{64,80},{80,96},{96,112},{112,128},... | collective-permute-start | bytes 2359304 | tf_op jit(solution)/shard_map/ppermute | solution.py:27
  53.9 85.6 %copy-start.2 = (bf16[1024,384]{1,0:T(8,128)(2,1)}, bf16[1024,384]{1,0:T(8,128)(2,1)S(1)}, u32[]{:S(2)}) copy-start(bf16[1024,384]{1,0:T(8,128)(2,1)S(1)} %collective-permute-done.8) | copy-start | bytes 2359300
  53.9 17.4 %collective-permute-start.9 = (bf16[1024,384]{1,0:T(8,128)(2,1)S(1)}, bf16[1024,384]{1,0:T(8,128)(2,1)}, u32[]{:S(2)}, u32[]{:S(2)}) collective-permute-start(bf16[1024,384]{1,0:T(8,128)(2,1)S(1)} %collective-permute-done.8), channel_id=1, source_target_pairs={{16,0},{32,16},{48,32},{64,48},{80,64},{96,80},{112,96},{128,112},... | collective-permute-start | bytes 2359304 | tf_op jit(solution)/shard_map/ppermute | solution.py:29
  66.5 17.7 %collective-permute-start.3 = (bf16[1024,384]{1,0:T(8,128)(2,1)}, bf16[1024,384]{1,0:T(8,128)(2,1)}, u32[]{:S(2)}, u32[]{:S(2)}) collective-permute-start(bf16[1024,384]{1,0:T(8,128)(2,1)} %collective-permute-done.2), channel_id=1, source_target_pairs={{0,16},{16,32},{32,48},{48,64},{64,80},{80,96},{96,112},{112,128},... | collective-permute-start | bytes 2359304 | tf_op jit(solution)/shard_map/ppermute | solution.py:27
  67.7 336.9 %reduce-scatter.2.cloned.1.call-start = ((), (), s32[]{:S(2)}) async-start(), calls=%async_computation.1 | async-start | bytes 1769472 | tf_op jit(solution)/shard_map/reduce_scatter | solution.py:172
  71.3 17.5 %collective-permute-start.10 = (bf16[1024,384]{1,0:T(8,128)(2,1)}, bf16[1024,384]{1,0:T(8,128)(2,1)S(1)}, u32[]{:S(2)}, u32[]{:S(2)}) collective-permute-start(bf16[1024,384]{1,0:T(8,128)(2,1)} %collective-permute-done.9), channel_id=1, source_target_pairs={{16,0},{32,16},{48,32},{64,48},{80,64},{96,80},{112,96},{128,112},... | collective-permute-start | bytes 2359304 | tf_op jit(solution)/shard_map/ppermute | solution.py:29
  84.2 19.5 %collective-permute-start.4 = (bf16[1024,384]{1,0:T(8,128)(2,1)}, bf16[1024,384]{1,0:T(8,128)(2,1)S(1)}, u32[]{:S(2)}, u32[]{:S(2)}) collective-permute-start(bf16[1024,384]{1,0:T(8,128)(2,1)} %collective-permute-done.3), channel_id=1, source_target_pairs={{0,16},{16,32},{32,48},{48,64},{64,80},{80,96},{96,112},{112,128},... | collective-permute-start | bytes 2359304 | tf_op jit(solution)/shard_map/ppermute | solution.py:27
  89.7 20.4 %collective-permute-start.11 = (bf16[1024,384]{1,0:T(8,128)(2,1)S(1)}, bf16[1024,384]{1,0:T(8,128)(2,1)S(1)}, u32[]{:S(2)}, u32[]{:S(2)}) collective-permute-start(bf16[1024,384]{1,0:T(8,128)(2,1)S(1)} %collective-permute-done.10), channel_id=1, source_target_pairs={{16,0},{32,16},{48,32},{64,48},{80,64},{96,80},{112,96},{128,112},... | collective-permute-start | bytes 2359304 | tf_op jit(solution)/shard_map/ppermute | solution.py:29
  103.7 23.8 %copy-start.9 = (bf16[1024,384]{1,0:T(8,128)(2,1)}, bf16[1024,384]{1,0:T(8,128)(2,1)S(1)}, u32[]{:S(2)}) copy-start(bf16[1024,384]{1,0:T(8,128)(2,1)S(1)} %collective-permute-done.4) | copy-start | bytes 2359300
  103.7 16.0 %collective-permute-start.5 = (bf16[1024,384]{1,0:T(8,128)(2,1)S(1)}, bf16[1024,384]{1,0:T(8,128)(2,1)S(1)}, u32[]{:S(2)}, u32[]{:S(2)}) collective-permute-start(bf16[1024,384]{1,0:T(8,128)(2,1)S(1)} %collective-permute-done.4), channel_id=1, source_target_pairs={{0,16},{16,32},{32,48},{48,64},{64,80},{80,96},{96,112},{112,128},... | collective-permute-start | bytes 2359304 | tf_op jit(solution)/shard_map/ppermute | solution.py:27
  111.0 16.4 %collective-permute-start.12 = (bf16[1024,384]{1,0:T(8,128)(2,1)S(1)}, bf16[1024,384]{1,0:T(8,128)(2,1)}, u32[]{:S(2)}, u32[]{:S(2)}) collective-permute-start(bf16[1024,384]{1,0:T(8,128)(2,1)S(1)} %collective-permute-done.11), channel_id=1, source_target_pairs={{16,0},{32,16},{48,32},{64,48},{80,64},{96,80},{112,96},{128,112},... | collective-permute-start | bytes 2359304 | tf_op jit(solution)/shard_map/ppermute | solution.py:29
  119.7 17.1 %collective-permute-start.6 = (bf16[1024,384]{1,0:T(8,128)(2,1)S(1)}, bf16[1024,384]{1,0:T(8,128)(2,1)}, u32[]{:S(2)}, u32[]{:S(2)}) collective-permute-start(bf16[1024,384]{1,0:T(8,128)(2,1)S(1)} %collective-permute-done.5), channel_id=1, source_target_pairs={{0,16},{16,32},{32,48},{48,64},{64,80},{80,96},{96,112},{112,128},... | collective-permute-start | bytes 2359304 | tf_op jit(solution)/shard_map/ppermute | solution.py:27
  127.5 69.0 %collective-permute-start.13 = (bf16[1024,384]{1,0:T(8,128)(2,1)}, bf16[1024,384]{1,0:T(8,128)(2,1)}, u32[]{:S(2)}, u32[]{:S(2)}) collective-permute-start(bf16[1024,384]{1,0:T(8,128)(2,1)} %collective-permute-done.12), channel_id=1, source_target_pairs={{16,0},{32,16},{48,32},{64,48},{80,64},{96,80},{112,96},{128,112},... | collective-permute-start | bytes 2359304 | tf_op jit(solution)/shard_map/ppermute | solution.py:29
  136.8 61.1 %collective-permute-start.7 = (bf16[1024,384]{1,0:T(8,128)(2,1)}, bf16[1024,384]{1,0:T(8,128)(2,1)}, u32[]{:S(2)}, u32[]{:S(2)}) collective-permute-start(bf16[1024,384]{1,0:T(8,128)(2,1)} %collective-permute-done.6), channel_id=1, source_target_pairs={{0,16},{16,32},{32,48},{48,64},{64,80},{80,96},{96,112},{112,128},... | collective-permute-start | bytes 2359304 | tf_op jit(solution)/shard_map/ppermute | solution.py:27
  196.5 28.7 %collective-permute-start.14 = (bf16[1024,384]{1,0:T(8,128)(2,1)}, bf16[1024,384]{1,0:T(8,128)(2,1)S(1)}, u32[]{:S(2)}, u32[]{:S(2)}) collective-permute-start(bf16[1024,384]{1,0:T(8,128)(2,1)} %collective-permute-done.13), channel_id=1, source_target_pairs={{16,0},{32,16},{48,32},{64,48},{80,64},{96,80},{112,96},{128,112},... | collective-permute-start | bytes 2359304 | tf_op jit(solution)/shard_map/ppermute | solution.py:29
  237.6 79.0 %copy-start.12 = (s32[1,128]{1,0:T(1,128)S(1)}, s32[1,128]{1,0:T(1,128)}, u32[]{:S(2)}) copy-start(s32[1,128]{1,0:T(1,128)} %param.15) | copy-start | bytes 1540
  237.6 80.9 %copy-start.11 = (f32[1,1024]{1,0:T(1,128)S(1)}, f32[1,1024]{1,0:T(1,128)}, u32[]{:S(2)}) copy-start(f32[1,1024]{1,0:T(1,128)} %param.16) | copy-start | bytes 12292
  404.5 6.0 %collective-permute-start.15 = (bf16[128,768]{1,0:T(8,128)(2,1)}, bf16[128,768]{1,0:T(8,128)(2,1)S(1)}, u32[]{:S(2)}, u32[]{:S(2)}) collective-permute-start(bf16[128,768]{1,0:T(8,128)(2,1)} %reduce-scatter.2.cloned.1.call-done), channel_id=1, source_target_pairs={{0,1},{1,0},{2,3},{3,2},{4,5},{5,4},{6,7},{7,6},{8,9},{9,8},{10,11... | collective-permute-start | bytes 589832 | tf_op jit(solution)/shard_map/ppermute | solution.py:61
  (7 other events, 82.0 us)
Sparse Core Ops, SparseCore 0:
  67.8 118.9 all-gather.3
  328.9 75.5 reduce-scatter.1
